TPU v7x, 128 devices: a whole 4x4x4 slice. The times are simulated.
128 devices in a mesh: role: 2 (over core), rows: 16 (over z, y), heads: 4 (over x).
Axes of the slice: x: 4, y: 4, z: 4, core: 2. Of those that a mesh axis runs over, the one named last changes fastest.
Arguments:
- queries: bfloat16 [512, 2, 4, 1024], P('rows', 'role', 'heads'), may hold values from -9 to 9
- k_cache: bfloat16 [512, 4, 512, 128], P('rows', 'heads'), may hold values from -6 to 6
- value_cache: bfloat16 [512, 4, 512, 128], P('rows', 'heads'), may hold values from -6 to 6
- new_token_key: bfloat16 [512, 4, 128], P('rows', 'heads'), may hold values from -6 to 6
- new_token_value: bfloat16 [512, 4, 128], P('rows', 'heads'), may hold values from -6 to 6
- lengths: int32 [512], P('rows'), may hold values from 2 to 512, as said below
- output_weight: bfloat16 [2, 4, 1024, 4096], P('role', 'heads'), may hold values from -0.5 to 0.5
- residual: bfloat16 [512, 4096], P('rows'), may hold values from -60 to 60
- norm_gain: float32 [4096], replicated, may hold values from 0.5 to 2
- routes: int32 [512, 8], P('rows'), may hold values from 0 to 63, all different within a row; in each aligned block of 32 rows (0 to 31, 32 to 63, ...) at most 8 rows name the same one
- route_scores: float32 [512, 8], P('rows'), may hold values from 0.05 to 1
- w_gate: bfloat16 [64, 4096, 1024], P(('role', 'rows'), None, 'heads'), may hold values from -0.09375 to 0.09375
- w_up: bfloat16 [64, 4096, 1024], P(('role', 'rows'), None, 'heads'), may hold values from -0.09375 to 0.09375
- w_down: bfloat16 [64, 1024, 4096], P(('role', 'rows'), 'heads'), may hold values from -0.1875 to 0.1875
Outputs:
- final: bfloat16 [512, 4096], P('rows', ('role', 'heads'))
Inputs may be any that keep to these rules, and one draw needn't show every extreme that they name: `lengths`: at least one row holds 512 cached positions. `routes`: each row names 8 different experts; the 32 rows of one index of rows name no expert more than 8 times, a bound that some block reaches.
All inputs are finite; a program needn't handle non-finite values.
Results may differ from a plain program's by a relative error of at most 0.015.
Values may be sent and summed in bfloat16 or wider, within the bound.
No kernel may reach another device: no remote copies, remote signals or barrier semaphores. Data moves between devices by JAX's collectives and lax.ppermute only.
A program may use at most 128 MiB of HBM per device.

v0:
```python
import math
import jax
import jax.numpy as jnp
from jax import lax
from jax.sharding import PartitionSpec as P


def per_device(
    queries,
    k_cache,
    value_cache,
    new_token_key,
    new_token_value,
    lengths,
    output_weight,
    residual,
    norm_gain,
    routes,
    route_scores,
    w_gate,
    w_up,
    w_down,
):
    rows_here = queries.shape[0]
    head_size = k_cache.shape[3]
    cache_len = k_cache.shape[2]
    per_group = queries.shape[3] // head_size
    root = math.sqrt(head_size)
    query_vectors = queries[:, 0, 0].reshape(rows_here, per_group, head_size)
    key_rows = k_cache[:, 0]
    value_rows = value_cache[:, 0]
    scores = (
        jnp.einsum("rqd,rld->rql", query_vectors, key_rows, preferred_element_type=jnp.float32)
        / root
    )
    fresh = (
        jnp.einsum(
            "rqd,rd->rq", query_vectors, new_token_key[:, 0], preferred_element_type=jnp.float32
        )
        / root
    )
    valid = lax.broadcasted_iota(jnp.int32, (rows_here, cache_len), 1) < lengths[:, None]
    scores = jnp.where(valid[:, None, :], scores, -jnp.inf)
    top = jnp.maximum(jnp.max(scores, axis=-1), fresh)
    expo = jnp.exp(scores - top[..., None])
    expo_new = jnp.exp(fresh - top)
    denom = jnp.sum(expo, axis=-1) + expo_new
    probs = (expo / denom[..., None]).astype(jnp.bfloat16)
    probs_new = (expo_new / denom).astype(jnp.bfloat16)
    attention_result = jnp.einsum(
        "rql,rld->rqd", probs, value_rows, preferred_element_type=jnp.float32
    )
    attention_result = (
        attention_result
        + probs_new.astype(jnp.float32)[..., None]
        * new_token_value[:, 0].astype(jnp.float32)[:, None, :]
    )
    attention_result = attention_result.astype(jnp.bfloat16).reshape(
        rows_here, per_group * head_size
    )
    partial_out = jnp.dot(attention_result, output_weight[0, 0], preferred_element_type=jnp.float32)
    width = residual.shape[1]
    roles = lax.axis_size("role")
    heads_count = lax.axis_size("heads")
    piece = width // (roles * heads_count)
    head_place = lax.axis_index("heads")
    place = lax.axis_index("role") * heads_count + head_place
    total = lax.psum(partial_out.astype(jnp.bfloat16), ("role", "heads")).astype(jnp.float32)
    hidden = residual.astype(jnp.float32) + total
    meansq = jnp.mean(hidden * hidden, axis=1, keepdims=True)
    normed = (hidden * lax.rsqrt(meansq + 1e-06) * norm_gain).astype(jnp.bfloat16)
    hidden_part = lax.dynamic_slice_in_dim(hidden, place * piece, piece, 1)
    top_k = routes.shape[1]
    per_dev = w_gate.shape[0]
    shards = lax.axis_size("rows")
    experts = per_dev * shards * roles
    capacity = max(2, 2 * rows_here * top_k // experts)
    slots = shards * per_dev * capacity
    picks = rows_here * top_k
    flat = routes.reshape(picks)
    order = jnp.arange(picks, dtype=jnp.int32)
    earlier = jnp.sum(
        ((flat[None, :] == flat[:, None]) & (order[None, :] < order[:, None])).astype(jnp.int32),
        axis=1,
    )
    owner = flat // (per_dev * shards)
    target = flat // per_dev % shards
    local = flat % per_dev
    slot_id = jnp.where(
        owner == lax.axis_index("role"), (target * per_dev + local) * capacity + earlier, -1
    )
    table = (slot_id[None, :] == jnp.arange(slots, dtype=jnp.int32)[:, None]).reshape(
        slots, rows_here, top_k
    )
    pick_rows = jnp.any(table, axis=2).astype(jnp.bfloat16)
    shares = route_scores / jnp.sum(route_scores, axis=1, keepdims=True)
    mixing = jnp.sum(jnp.where(table, shares[None, :, :], jnp.float32(0.0)), axis=2).T
    outgoing = jnp.dot(pick_rows, normed, preferred_element_type=jnp.float32).astype(jnp.bfloat16)
    outgoing = outgoing.reshape(shards, per_dev, capacity, width)
    incoming = lax.all_to_all(outgoing, "rows", split_axis=0, concat_axis=0, tiled=True)
    gate = jnp.einsum("secd,edf->secf", incoming, w_gate, preferred_element_type=jnp.float32)
    upper = jnp.einsum("secd,edf->secf", incoming, w_up, preferred_element_type=jnp.float32)
    act = (jax.nn.silu(gate) * upper).astype(jnp.bfloat16)
    result = jnp.einsum("secf,efd->secd", act, w_down, preferred_element_type=jnp.float32).astype(
        jnp.bfloat16
    )
    returned = lax.all_to_all(result, "rows", split_axis=0, concat_axis=0, tiled=True)
    flat_back = returned.reshape(slots, width)
    mix_high = mixing.astype(jnp.bfloat16)
    mix_low = (mixing - mix_high.astype(jnp.float32)).astype(jnp.bfloat16)
    mixed = jnp.dot(mix_high, flat_back, preferred_element_type=jnp.float32) + jnp.dot(
        mix_low, flat_back, preferred_element_type=jnp.float32
    )
    moe = lax.psum_scatter(
        mixed.astype(jnp.bfloat16), ("role", "heads"), scatter_dimension=1, tiled=True
    ).astype(jnp.float32)
    return (hidden_part + moe).astype(jnp.bfloat16)


def solution(mesh):
    in_specs = (
        P("rows", "role", "heads", None),
        P("rows", "heads", None, None),
        P("rows", "heads", None, None),
        P("rows", "heads", None),
        P("rows", "heads", None),
        P("rows"),
        P("role", "heads", None, None),
        P("rows", None),
        P(),
        P("rows", None),
        P("rows", None),
        P(("role", "rows"), None, "heads"),
        P(("role", "rows"), None, "heads"),
        P(("role", "rows"), "heads", None),
    )
    out_specs = P("rows", ("role", "heads"))
    return jax.shard_map(
        per_device, mesh=mesh, in_specs=in_specs, out_specs=out_specs, check_vma=False
    )
```

profile of v0, /device:TPU:1, one launch (start us, length us, event | category | flops | bytes accessed | tf_op | source)
XLA Modules:
  0.0 201.6 jit_solution(10474719294296749391)
XLA Ops:
  6.5 0.9 copy.49
  7.4 0.7 iota_compare_fusion.2
  8.2 0.1 fusion.79
  8.3 0.0 copy-start.1
  8.3 3.6 %fusion.88 = (f32[32,8]{1,0:T(8,128)S(1)}, f32[32,8,512]{2,1,0:T(8,128)S(1)}) fusion(bf16[32,8,128]{2,1,0:T(8,128)(2,1)S(1)} %bitcast.106, bf16[32,1,512,128]{3,2,1,0:T(8,128)(2,1)} %param.15, pred[32,512]{1,0:T(8,128)(4,1)S(1)} %iota_compare_fusion.2), kind=kOutput, calls=%fused_computation.90 | convolution fusion | flops 33947392 | bytes 4801536 | tf_op jit(solution)/shard_map/rqd,rld->rql/dot_general | solution.py:33
  11.9 0.2 fusion.50
  12.2 2.9 %fusion.47 = bf16[32,8,128]{2,1,0:T(8,128)(2,1)S(1)} fusion(bf16[32,1,512,128]{3,2,1,0:T(8,128)(2,1)} %param.16, f32[32,8,512]{2,1,0:T(8,128)S(1)} %get-tuple-element.10, f32[32,8]{1,0:T(8,128)S(1)} %get-tuple-element.8, f32[32,8]{1,0:T(8,128)S(1)} %multiply_maximum_fusion, f32[32,128]{1,0:T(8,128)S(1)} %bitcast_convert_fusion.3, ...), kind=kOutput, calls=%fused_computation.26 | convolution fusion | flops 34045952 | bytes 4803584 | tf_op jit(solution)/shard_map/rql,rld->rqd/dot_general | solution.py:50
  15.2 2.2 %fusion.4 = bf16[32,4096]{1,0:T(8,128)(2,1)} fusion(bf16[1,1,1024,4096]{3,2,1,0:T(8,128)(2,1)S(1)} %copy-done.1, bf16[4,8,8,128]{3,2,1,0:T(8,128)(2,1)S(1)} %bitcast.104), kind=kOutput, calls=%fused_computation.7 | convolution fusion | flops 268566528 | bytes 8716288 | tf_op jit(solution)/shard_map/dot_general | solution.py:61
  17.4 0.0 all-reduce.2.cloned.1.call-update
  17.5 0.1 copy.35
  17.6 0.1 eq.42
  17.6 0.2 convert_reduce_fusion
  17.8 0.1 reduce_sum.49
  17.9 0.1 fusion.77
  18.0 0.2 fusion.62
  18.1 60.4 %all-reduce.2.cloned.1.call-done = bf16[32,4096]{1,0:T(8,128)(2,1)} async-done(((bf16[32,4096]{1,0:T(8,128)(2,1)}), bf16[32,4096]{1,0:T(8,128)(2,1)}) %all-reduce.2.cloned.1.call-update) | async-done | bytes 262160 | tf_op jit(solution)/shard_map/psum | solution.py:68
  78.5 1.3 convert_add_fusion
  79.8 1.7 convolution_convert_fusion.1
  81.6 31.8 %all_to_all.10 = bf16[16,2,8,4096]{3,2,1,0:T(8,128)(2,1)S(1)} all-to-all(bf16[16,2,8,4096]{3,2,1,0:T(8,128)(2,1)S(1)} %bitcast.103), channel_id=1, replica_groups=mesh['role'=2,'rows'=16,'heads'=4] {'rows'}, dimensions={0} | all-to-all | bytes 4194304 | tf_op jit(solution)/shard_map/all_to_all | solution.py:100
  113.4 0.8 fusion.24
  114.1 6.3 %fusion.2 = bf16[16,2,8,4096]{3,2,0,1:T(8,128)(2,1)} fusion(bf16[2,256,4096]{2,1,0:T(8,128)(2,1)} %param.27, bf16[2,4096,256]{2,1,0:T(8,128)(2,1)} %param.26, bf16[16,2,8,4096]{3,2,1,0:T(8,128)(2,1)S(1)} %all_to_all.10, f32[16,2,8,256]{3,2,0,1:T(8,128)S(1)} %fusion.24), kind=kOutput, calls=%fused_computation.4 | convolution fusion | flops 1075183616 | bytes 12845056 | tf_op jit(solution)/shard_map/secf,efd->secd/dot_general | solution.py:104
  120.4 3.1 %copy.43 = bf16[16,2,8,4096]{3,2,1,0:T(8,128)(2,1)} copy(bf16[16,2,8,4096]{3,2,0,1:T(8,128)(2,1)} %fusion.2) | data formatting | bytes 4194304 | tf_op jit(solution)/shard_map/convert_element_type | solution.py:104
  123.5 3.7 %all-to-all-start.1 = ((bf16[16,2,8,4096]{3,2,1,0:T(8,128)(2,1)}), bf16[16,2,8,4096]{3,2,1,0:T(8,128)(2,1)S(1)}, u32[]{:S(2)}, u32[]{:S(2)}) async-start(bf16[16,2,8,4096]{3,2,1,0:T(8,128)(2,1)} %copy.43), calls=%async_computation.1 | async-start | bytes 4194304 | tf_op jit(solution)/shard_map/all_to_all | solution.py:107
  127.3 0.0 reduce-scatter.2.cloned.1.call-start
  127.4 0.1 copy.40
  127.4 0.2 select_reduce_fusion
  127.6 24.4 %all-to-all-done.1 = bf16[16,2,8,4096]{3,2,1,0:T(8,128)(2,1)S(1)} async-done(((bf16[16,2,8,4096]{3,2,1,0:T(8,128)(2,1)}), bf16[16,2,8,4096]{3,2,1,0:T(8,128)(2,1)S(1)}, u32[]{:S(2)}, u32[]{:S(2)}) %all-to-all-start.1) | async-done | bytes 2097184 | tf_op jit(solution)/shard_map/all_to_all | solution.py:107
  152.0 0.5 fusion.89
  152.5 1.2 fusion.3
  153.7 0.0 reduce-scatter.2.cloned.1.call-update
  153.7 39.7 %reduce-scatter.2.cloned.1.call-done = bf16[32,512]{1,0:T(8,128)(2,1)} async-done(((bf16[32,4096]{1,0:T(8,128)(2,1)}), bf16[32,512]{1,0:T(8,128)(2,1)}) %reduce-scatter.2.cloned.1.call-update) | async-done | bytes 32784 | tf_op jit(solution)/shard_map/reduce_scatter | solution.py:114
  193.4 1.4 add_convert_fusion
  (22 shorter events, 0.1 us)
Async XLA Ops:
  6.5 1.6 copy-start
  6.5 5.7 %copy-start.6 = (bf16[32,1,128]{2,0,1:T(8,128)(2,1)S(1)}, bf16[32,1,128]{2,0,1:T(8,128)(2,1)}, u32[]{:S(2)}) copy-start(bf16[32,1,128]{2,0,1:T(8,128)(2,1)} %param.18) | copy-start | bytes 24580
  6.5 71.9 %all-reduce.2.cloned.1.call-start = ((), (), s32[]{:S(2)}) async-start(), calls=%async_computation.3 | async-start | bytes 524288 | tf_op jit(solution)/shard_map/psum | solution.py:68
  8.3 6.8 %copy-start.1 = (bf16[1,1,1024,4096]{3,2,1,0:T(8,128)(2,1)S(1)}, bf16[1,1,1024,4096]{3,2,1,0:T(8,128)(2,1)}, u32[]{:S(2)}) copy-start(bf16[1,1,1024,4096]{3,2,1,0:T(8,128)(2,1)} %param.20) | copy-start | bytes 25165828
  15.1 2.3 %copy-start.7 = (s32[32,8]{0,1:T(8,128)S(1)}, s32[32,8]{0,1:T(8,128)}, u32[]{:S(2)}) copy-start(s32[32,8]{0,1:T(8,128)} %param.23) | copy-start | bytes 3076
  15.2 63.3 %copy-start.3 = (bf16[32,4096]{1,0:T(8,128)(2,1)S(1)}, bf16[32,4096]{1,0:T(8,128)(2,1)}, u32[]{:S(2)}) copy-start(bf16[32,4096]{1,0:T(8,128)(2,1)} %param.21) | copy-start | bytes 786436
  15.2 64.6 %copy-start.4 = (f32[4096]{0:T(1024)S(1)}, f32[4096]{0:T(1024)}, u32[]{:S(2)}) copy-start(f32[4096]{0:T(1024)} %param.22) | copy-start | bytes 49156
  78.5 34.9 %copy-start.2 = (bf16[2,4096,256]{2,1,0:T(8,128)(2,1)S(1)}, bf16[2,4096,256]{2,1,0:T(8,128)(2,1)}, u32[]{:S(2)}) copy-start(bf16[2,4096,256]{2,1,0:T(8,128)(2,1)} %param.25) | copy-start | bytes 12582916
  120.4 6.9 %copy-start.5 = (f32[32,8]{0,1:T(8,128)S(1)}, f32[32,8]{0,1:T(8,128)}, u32[]{:S(2)}) copy-start(f32[32,8]{0,1:T(8,128)} %param.24) | copy-start | bytes 3076
  123.5 28.5 %all-to-all-start.1 = ((bf16[16,2,8,4096]{3,2,1,0:T(8,128)(2,1)}), bf16[16,2,8,4096]{3,2,1,0:T(8,128)(2,1)S(1)}, u32[]{:S(2)}, u32[]{:S(2)}) async-start(bf16[16,2,8,4096]{3,2,1,0:T(8,128)(2,1)} %copy.43), calls=%async_computation.1 | async-start | bytes 4194304 | tf_op jit(solution)/shard_map/all_to_all | solution.py:107
  127.3 66.1 %reduce-scatter.2.cloned.1.call-start = ((), (), s32[]{:S(2)}) async-start(), calls=%async_computation.4 | async-start | bytes 294912 | tf_op jit(solution)/shard_map/reduce_scatter | solution.py:114
Sparse Core Ops, SparseCore 0:
  17.6 60.8 all-reduce.1
  153.8 39.5 reduce-scatter.1
where the time goes:
time: 202 us
  waiting for transfers between devices  124 us (61%)
  blocking collectives  31.8 us (16%)
  matrix products  19.3 us (10%)
  between operations  13.6 us (7%)
  local copies, waits for them, and re-layouts  4.36 us (2%)
  other arithmetic  4.28 us (2%)
  starting transfers between devices  3.76 us (2%)
    psum x1, waiting for transfers between devices, per_device(): lax.psum(partial_out.astype(jnp.bfloat16), ('role', 'heads'))  60.4 us
    reduce_scatter x1, waiting for transfers between devices, per_device(): lax.psum_scatter(mixed.astype(jnp.bfloat16), ('role', 'heads'), scatter_d...  39.7 us
    all_to_all x1, blocking collectives, per_device(): lax.all_to_all(outgoing, 'rows', split_axis=0, concat_axis=0, tiled=True)  31.8 us
    all_to_all x1, waiting for transfers between devices, per_device(): lax.all_to_all(result, 'rows', split_axis=0, concat_axis=0, tiled=True)  24.4 us
    dot_general x1, matrix products, per_device(): jnp.einsum('secf,efd->secd', act, w_down, preferred_element_type=jnp.floa...  6.3 us
  transfers between devices with their start and end apart: 3, of which 3 were waited for; matrix products, arithmetic and copies ran while one was open for 0% of the time, Pallas kernels for 0%

commit v1 on v0

--- a/solution.py
+++ b/solution.py
@@ -65,7 +65,9 @@
     piece = width // (roles * heads_count)
     head_place = lax.axis_index("heads")
     place = lax.axis_index("role") * heads_count + head_place
-    total = lax.psum(partial_out.astype(jnp.bfloat16), ("role", "heads")).astype(jnp.float32)
+    total = jnp.sum(
+        lax.all_gather(partial_out.astype(jnp.bfloat16), ("role", "heads")), axis=0
+    ).astype(jnp.float32)
     hidden = residual.astype(jnp.float32) + total
     meansq = jnp.mean(hidden * hidden, axis=1, keepdims=True)
     normed = (hidden * lax.rsqrt(meansq + 1e-06) * norm_gain).astype(jnp.bfloat16)

time: 202 us -> 167 us (0.83)
  waiting for transfers between devices: 124 us -> 87.2 us
  blocking collectives: 31.8 us -> 34.3 us
    psum x1 -> x0, waiting for transfers between devices: 60.4 us -> none  [per_device(): lax.psum(partial_out.astype(jnp.bfloat16), ('role', 'heads'))]
    all_gather x0 -> x1, waiting for transfers between devices: none -> 28.2 us  [per_device(): lax.all_gather(partial_out.astype(jnp.bfloat16), ('role', 'heads'))]
    reduce_scatter x1, waiting for transfers between devices: 39.7 us -> 31 us  [per_device(): lax.psum_scatter(mixed.astype(jnp.bfloat16), ('role', 'heads'), scatter_d...]
    all_to_all x1, waiting for transfers between devices: 24.4 us -> 27.9 us  [per_device(): lax.all_to_all(result, 'rows', split_axis=0, concat_axis=0, tiled=True)]
    all_to_all x1, blocking collectives: 31.8 us -> 34.3 us  [per_device(): lax.all_to_all(outgoing, 'rows', split_axis=0, concat_axis=0, tiled=True)]
  transfers between devices with their start and end apart: 3 -> 3, of which waited for: 3 -> 3; matrix products, arithmetic and copies ran while one was open for 0% -> 1% of each run, Pallas kernels for 0% -> 0%
where the time goes in v1:
time: 167 us
  waiting for transfers between devices  87.2 us (52%)
  blocking collectives  34.3 us (21%)
  matrix products  18.4 us (11%)
  between operations  13.6 us (8%)
  other arithmetic  5.1 us (3%)
  local copies, waits for them, and re-layouts  4.36 us (3%)
  starting transfers between devices  3.76 us (2%)
    all_to_all x1, blocking collectives, per_device(): lax.all_to_all(outgoing, 'rows', split_axis=0, concat_axis=0, tiled=True)  34.3 us
    reduce_scatter x1, waiting for transfers between devices, per_device(): lax.psum_scatter(mixed.astype(jnp.bfloat16), ('role', 'heads'), scatter_d...  31 us
    all_gather x1, waiting for transfers between devices, per_device(): lax.all_gather(partial_out.astype(jnp.bfloat16), ('role', 'heads'))  28.2 us
    all_to_all x1, waiting for transfers between devices, per_device(): lax.all_to_all(result, 'rows', split_axis=0, concat_axis=0, tiled=True)  27.9 us
    dot_general x1, matrix products, per_device(): jnp.einsum('secf,efd->secd', act, w_down, preferred_element_type=jnp.floa...  6.3 us
    all_to_all x1, starting transfers between devices, per_device(): lax.all_to_all(result, 'rows', split_axis=0, concat_axis=0, tiled=True)  3.72 us
    dot_general x1, matrix products, per_device(): jnp.einsum('rqd,rld->rql', query_vectors, key_rows, preferred_element_typ...  3.61 us
  transfers between devices with their start and end apart: 3, of which 3 were waited for; matrix products, arithmetic and copies ran while one was open for 1% of the time, Pallas kernels for 0%

profile of v1, /device:TPU:1, one launch (start us, length us, event | category | flops | bytes accessed | tf_op | source)
XLA Modules:
  0.0 166.7 jit_solution(1091540663723128069)
XLA Ops:
  6.5 0.9 copy.49
  7.4 0.7 iota_compare_fusion.2
  8.2 0.1 fusion.79
  8.3 3.6 %fusion.88 = (f32[32,8]{1,0:T(8,128)S(1)}, f32[32,8,512]{2,1,0:T(8,128)S(1)}) fusion(bf16[32,8,128]{2,1,0:T(8,128)(2,1)S(1)} %bitcast.108, bf16[32,1,512,128]{3,2,1,0:T(8,128)(2,1)} %param.15, pred[32,512]{1,0:T(8,128)(4,1)S(1)} %iota_compare_fusion.2), kind=kOutput, calls=%fused_computation.90 | convolution fusion | flops 33947392 | bytes 4801536 | tf_op jit(solution)/shard_map/rqd,rld->rql/dot_general | solution.py:33
  11.9 0.2 fusion.50
  12.2 2.9 %fusion.47 = bf16[32,8,128]{2,1,0:T(8,128)(2,1)S(1)} fusion(bf16[32,1,512,128]{3,2,1,0:T(8,128)(2,1)} %param.16, f32[32,8,512]{2,1,0:T(8,128)S(1)} %get-tuple-element.10, f32[32,8]{1,0:T(8,128)S(1)} %get-tuple-element.8, f32[32,8]{1,0:T(8,128)S(1)} %multiply_maximum_fusion, f32[32,128]{1,0:T(8,128)S(1)} %bitcast_convert_fusion.3, ...), kind=kOutput, calls=%fused_computation.26 | convolution fusion | flops 34045952 | bytes 4803584 | tf_op jit(solution)/shard_map/rql,rld->rqd/dot_general | solution.py:50
  15.2 2.3 %fusion.4 = bf16[32,4096]{1,0:T(8,128)(2,1)} fusion(bf16[1,1,1024,4096]{3,2,1,0:T(8,128)(2,1)S(1)} %copy-done.1, bf16[4,8,8,128]{3,2,1,0:T(8,128)(2,1)S(1)} %bitcast.106), kind=kOutput, calls=%fused_computation.7 | convolution fusion | flops 268566528 | bytes 8716288 | tf_op jit(solution)/shard_map/dot_general | solution.py:61
  17.5 0.0 all-gather.3.cloned.1.call-update
  17.5 0.1 copy.35
  17.6 0.1 eq.42
  17.7 0.2 convert_reduce_fusion
  17.9 0.1 reduce_sum.62
  17.9 0.1 fusion.77
  18.0 0.2 fusion.62
  18.2 28.2 %all-gather.3.cloned.1.call-done = bf16[256,4096]{1,0:T(8,128)(2,1)} async-done(((bf16[32,4096]{1,0:T(8,128)(2,1)}), bf16[256,4096]{1,0:T(8,128)(2,1)}) %all-gather.3.cloned.1.call-update) | async-done | bytes 2097168 | tf_op jit(solution)/shard_map/all_gather | solution.py:69
  46.4 1.9 %reduce_sum.60 = bf16[32,4096]{1,0:T(8,128)(2,1)S(1)} reduce(bf16[8,32,4096]{2,1,0:T(8,128)(2,1)} %bitcast.105, bf16[]{:T(256)} %constant.70.clone.1), dimensions={0}, to_apply=%region_2.3 | reduce | flops 917504 | bytes 2359298 | tf_op jit(solution)/shard_map/reduce_sum | solution.py:68
  48.3 0.2 convert_add_fusion
  48.6 0.8 convolution_convert_fusion.1
  49.3 34.3 %all_to_all.10 = bf16[16,2,8,4096]{3,2,1,0:T(8,128)(2,1)S(1)} all-to-all(bf16[16,2,8,4096]{3,2,1,0:T(8,128)(2,1)S(1)} %bitcast.104), channel_id=1, replica_groups=mesh['role'=2,'rows'=16,'heads'=4] {'rows'}, dimensions={0} | all-to-all | bytes 4194304 | tf_op jit(solution)/shard_map/all_to_all | solution.py:102
  83.7 0.8 fusion.24
  84.4 6.3 %fusion.2 = bf16[16,2,8,4096]{3,2,0,1:T(8,128)(2,1)} fusion(bf16[2,256,4096]{2,1,0:T(8,128)(2,1)} %param.27, bf16[2,4096,256]{2,1,0:T(8,128)(2,1)} %param.26, bf16[16,2,8,4096]{3,2,1,0:T(8,128)(2,1)S(1)} %all_to_all.10, f32[16,2,8,256]{3,2,0,1:T(8,128)S(1)} %fusion.24), kind=kOutput, calls=%fused_computation.4 | convolution fusion | flops 1075183616 | bytes 12845056 | tf_op jit(solution)/shard_map/secf,efd->secd/dot_general | solution.py:106
  90.7 3.1 %copy.43 = bf16[16,2,8,4096]{3,2,1,0:T(8,128)(2,1)} copy(bf16[16,2,8,4096]{3,2,0,1:T(8,128)(2,1)} %fusion.2) | data formatting | bytes 4194304 | tf_op jit(solution)/shard_map/convert_element_type | solution.py:106
  93.8 3.7 %all-to-all-start.1 = ((bf16[16,2,8,4096]{3,2,1,0:T(8,128)(2,1)}), bf16[16,2,8,4096]{3,2,1,0:T(8,128)(2,1)S(1)}, u32[]{:S(2)}, u32[]{:S(2)}) async-start(bf16[16,2,8,4096]{3,2,1,0:T(8,128)(2,1)} %copy.43), calls=%async_computation.1 | async-start | bytes 4194304 | tf_op jit(solution)/shard_map/all_to_all | solution.py:109
  97.6 0.0 reduce-scatter.2.cloned.1.call-start
  97.7 0.1 copy.40
  97.7 0.2 select_reduce_fusion
  97.9 27.9 %all-to-all-done.1 = bf16[16,2,8,4096]{3,2,1,0:T(8,128)(2,1)S(1)} async-done(((bf16[16,2,8,4096]{3,2,1,0:T(8,128)(2,1)}), bf16[16,2,8,4096]{3,2,1,0:T(8,128)(2,1)S(1)}, u32[]{:S(2)}, u32[]{:S(2)}) %all-to-all-start.1) | async-done | bytes 2097184 | tf_op jit(solution)/shard_map/all_to_all | solution.py:109
  125.8 0.5 fusion.89
  126.3 1.2 fusion.3
  127.5 0.0 reduce-scatter.2.cloned.1.call-update
  127.5 31.0 %reduce-scatter.2.cloned.1.call-done = bf16[32,512]{1,0:T(8,128)(2,1)} async-done(((bf16[32,4096]{1,0:T(8,128)(2,1)}), bf16[32,512]{1,0:T(8,128)(2,1)}) %reduce-scatter.2.cloned.1.call-update) | async-done | bytes 32784 | tf_op jit(solution)/shard_map/reduce_scatter | solution.py:116
  158.5 1.4 add_convert_fusion
  (23 shorter events, 0.1 us)
Async XLA Ops:
  6.5 1.6 copy-start
  6.5 5.7 %copy-start.6 = (bf16[32,1,128]{2,0,1:T(8,128)(2,1)S(1)}, bf16[32,1,128]{2,0,1:T(8,128)(2,1)}, u32[]{:S(2)}) copy-start(bf16[32,1,128]{2,0,1:T(8,128)(2,1)} %param.18) | copy-start | bytes 24580
  6.5 39.9 %all-gather.3.cloned.1.call-start = ((), (), s32[]{:S(2)}) async-start(), calls=%async_computation.4 | async-start | bytes 2359296 | tf_op jit(solution)/shard_map/all_gather | solution.py:69
  8.3 6.8 %copy-start.1 = (bf16[1,1,1024,4096]{3,2,1,0:T(8,128)(2,1)S(1)}, bf16[1,1,1024,4096]{3,2,1,0:T(8,128)(2,1)}, u32[]{:S(2)}) copy-start(bf16[1,1,1024,4096]{3,2,1,0:T(8,128)(2,1)} %param.20) | copy-start | bytes 25165828
  15.1 2.3 %copy-start.7 = (s32[32,8]{0,1:T(8,128)S(1)}, s32[32,8]{0,1:T(8,128)}, u32[]{:S(2)}) copy-start(s32[32,8]{0,1:T(8,128)} %param.23) | copy-start | bytes 3076
  15.2 33.2 %copy-start.3 = (bf16[32,4096]{1,0:T(8,128)(2,1)S(1)}, bf16[32,4096]{1,0:T(8,128)(2,1)}, u32[]{:S(2)}) copy-start(bf16[32,4096]{1,0:T(8,128)(2,1)} %param.21) | copy-start | bytes 786436
  15.2 33.4 %copy-start.4 = (f32[4096]{0:T(1024)S(1)}, f32[4096]{0:T(1024)}, u32[]{:S(2)}) copy-start(f32[4096]{0:T(1024)} %param.22) | copy-start | bytes 49156
  48.3 35.3 %copy-start.2 = (bf16[2,4096,256]{2,1,0:T(8,128)(2,1)S(1)}, bf16[2,4096,256]{2,1,0:T(8,128)(2,1)}, u32[]{:S(2)}) copy-start(bf16[2,4096,256]{2,1,0:T(8,128)(2,1)} %param.25) | copy-start | bytes 12582916
  90.7 6.9 %copy-start.5 = (f32[32,8]{0,1:T(8,128)S(1)}, f32[32,8]{0,1:T(8,128)}, u32[]{:S(2)}) copy-start(f32[32,8]{0,1:T(8,128)} %param.24) | copy-start | bytes 3076
  93.8 32.0 %all-to-all-start.1 = ((bf16[16,2,8,4096]{3,2,1,0:T(8,128)(2,1)}), bf16[16,2,8,4096]{3,2,1,0:T(8,128)(2,1)S(1)}, u32[]{:S(2)}, u32[]{:S(2)}) async-start(bf16[16,2,8,4096]{3,2,1,0:T(8,128)(2,1)} %copy.43), calls=%async_computation.1 | async-start | bytes 4194304 | tf_op jit(solution)/shard_map/all_to_all | solution.py:109
  97.6 60.9 %reduce-scatter.2.cloned.1.call-start = ((), (), s32[]{:S(2)}) async-start(), calls=%async_computation.3 | async-start | bytes 294912 | tf_op jit(solution)/shard_map/reduce_scatter | solution.py:116
Sparse Core Ops, SparseCore 0:
  17.6 28.7 all-gather.2
  127.6 30.8 reduce-scatter.1
